TPU v7x, 256 devices: a whole 4x4x8 slice. The times are simulated.
256 devices in a mesh: space: 32 (over x, z), grp: 8 (over y, core).
Axes of the slice: x: 4, y: 4, z: 8, core: 2. Of those that a mesh axis runs over, the one named last changes fastest.
Arguments:
- trial: bfloat16 [32768, 512], P(('space', 'grp')), may hold values from -11 to 11, as said below
- support: int32 [256, 2], P(('space', 'grp')), may hold values 0 or 1
- density: bfloat16 [32768, 1024], P(('space', 'grp')), may hold values from -0.25 to 0.25
- density_pattern: int32 [256, 8], P(('space', 'grp')), may hold values 0 or 1
- margin: bfloat16 [32768, 3072], P(('space', 'grp')), may hold values from -1 to 1, as said below
- margin_pattern: int32 [256, 24], P(('space', 'grp')), may hold values from 0 to 1, as said below
- pair_pattern: int32 [32, 3, 2, 2], P('space'), may hold values from 0 to 1, as said below
Outputs:
- orthonormal: float32 [32768, 1536], P(('space', 'grp'))
Inputs may be any that keep to these rules, and one draw needn't show every extreme that they name: trial is a float array; its rows of later domains tend to be larger. margin, read with margin_pattern, is a symmetric matrix over all 32768 orbitals with unit diagonal. `margin_pattern`: symmetric between atom blocks over all domains; every atom block is paired with itself. `pair_pattern`: symmetric between trial blocks over all domains; every trial block is paired with itself.
All inputs are finite; a program needn't handle non-finite values. No bound on the sum of `support` or of `density_pattern` on one device may be relied on, other than what follows from the above.
Results may differ from a plain program's by a relative error of at most 0.004.
Values may be sent and summed in bfloat16 or wider, within the bound.
No kernel may reach another device: no remote copies, remote signals or barrier semaphores. Data moves between devices by JAX's collectives and lax.ppermute only.
A program may use at most 64 MiB of HBM per device.

v0:
```python
import jax
import jax.numpy as jnp
from jax import lax
from jax.sharding import PartitionSpec as P


def padded(array, sides, width):
    for axis, dim in sides:
        devices, length = (lax.axis_size(axis), array.shape[dim])
        up = [(i, (i + 1) % devices) for i in range(devices)]
        down = [(j, i) for i, j in up]
        last = lax.slice_in_dim(array, length - width, length, axis=dim)
        leading = lax.slice_in_dim(array, 0, width, axis=dim)
        before = lax.ppermute(last, axis, up)
        after = lax.ppermute(leading, axis, down)
        array = jnp.concatenate([before, array, after], axis=dim)
    return array


def matmul_high(left_side, right_side):
    return jnp.dot(
        left_side, right_side, precision=lax.Precision.HIGHEST, preferred_element_type=jnp.float32
    )


def space_sides(band):
    return padded(band, (("space", 0),), 2)


def widen_whole(band):
    return space_sides(band)


def band_product(left_side, right_side, widen):
    widened = widen(right_side)
    lower = matmul_high(left_side[0], widened[0]) + matmul_high(left_side[1], widened[2])
    center = (
        matmul_high(left_side[0], widened[1])
        + matmul_high(left_side[1], widened[3])
        + matmul_high(left_side[2], widened[5])
    )
    upper = matmul_high(left_side[1], widened[4]) + matmul_high(left_side[2], widened[6])
    return jnp.stack([lower, center, upper])


def per_device(trial, support, density, density_pattern, margin, margin_pattern, pair_pattern):
    row_count = trial.shape[0]
    atom_count = support.shape[0]
    atom_orbs = row_count // atom_count
    trial_count = support.shape[1]
    trial_cols = trial.shape[1]
    trial_width = trial_cols // trial_count
    dom_rows = density.shape[1]
    dom_atoms = density_pattern.shape[1]
    support_mask = support.astype(jnp.bfloat16).reshape(atom_count, 1, trial_count, 1)
    trial_eff = (
        trial.reshape(atom_count, atom_orbs, trial_count, trial_width) * support_mask
    ).reshape(row_count, trial_cols)
    density_mask = density_pattern.astype(jnp.bfloat16).reshape(atom_count, 1, dom_atoms, 1)
    density_eff = (
        density.reshape(atom_count, atom_orbs, dom_atoms, atom_orbs) * density_mask
    ).reshape(row_count, dom_rows)
    projected = jnp.dot(
        density_eff,
        lax.all_gather(trial_eff, "grp", axis=0, tiled=True),
        preferred_element_type=jnp.float32,
    ).astype(jnp.bfloat16)
    margin_mask = margin_pattern.astype(jnp.bfloat16).reshape(atom_count, 1, 3, dom_atoms, 1)
    margin_eff = (
        margin.reshape(atom_count, atom_orbs, 3, dom_atoms, atom_orbs) * margin_mask
    ).reshape(row_count, 3, dom_rows)
    domain_psi = lax.all_gather(projected, "grp", axis=0, tiled=True)
    nearby = padded(domain_psi[None], (("space", 0),), 1)
    applied = jnp.einsum("rjc,jct->jrt", margin_eff, nearby, preferred_element_type=jnp.float32)
    applied = applied.astype(jnp.bfloat16)
    partial_sums = jnp.einsum("rt,jru->jtu", projected, applied, preferred_element_type=jnp.float32)
    pair_local = pair_pattern[0].astype(jnp.float32).reshape(3, trial_count, 1, trial_count, 1)
    pair_mask = jnp.broadcast_to(
        pair_local, (3, trial_count, trial_width, trial_count, trial_width)
    ).reshape(3, trial_cols, trial_cols)
    identity = jnp.eye(trial_cols, dtype=jnp.float32)
    nothing = jnp.zeros_like(identity)
    identity_band = jnp.stack([nothing, identity, nothing])
    blocks = lax.psum(partial_sums, "grp") * pair_mask
    peak = lax.pmax(jnp.max(jnp.diagonal(blocks[1])), "space")
    scaled = blocks / peak
    z_one = pair_mask * (1.5 * identity_band - 0.5 * scaled)
    square = pair_mask * band_product(z_one, z_one, widen_whole)
    weighed = pair_mask * band_product(scaled, square, widen_whole)
    z_two = pair_mask * (1.5 * z_one - 0.5 * band_product(z_one, weighed, widen_whole))
    result = jnp.einsum(
        "rt,jtu->rju", projected.astype(jnp.float32), z_two, precision=lax.Precision.HIGHEST
    )
    return result.reshape(row_count, 3 * trial_cols)


def solution(mesh):
    placed = (
        P(("space", "grp"), None),
        P(("space", "grp"), None),
        P(("space", "grp"), None),
        P(("space", "grp"), None),
        P(("space", "grp"), None),
        P(("space", "grp"), None),
        P("space", None, None, None),
    )
    return jax.shard_map(
        per_device, mesh=mesh, in_specs=placed, out_specs=P(("space", "grp"), None), check_vma=False
    )
```

profile of v0, /device:TPU:24, one launch (start us, length us, event | category | flops | bytes accessed | tf_op | source)
XLA Modules:
  0.0 423.7 jit_solution(4265930637378047454)
XLA Ops:
  9.7 26.5 %all-gather.3.cloned.1.call-done = bf16[1024,512]{1,0:T(8,128)(2,1)} async-done(((bf16[128,512]{1,0:T(8,128)(2,1)}), bf16[1024,512]{1,0:T(8,128)(2,1)}) %all-gather.3.cloned.1.call-update) | async-done | bytes 1048592 | tf_op jit(solution)/shard_map/all_gather | solution.py:65
  36.2 2.3 convolution_convert_fusion
  38.5 25.9 %all-gather.5.cloned.1.call-done = bf16[1024,512]{1,0:T(8,128)(2,1)} async-done(((bf16[128,512]{1,0:T(8,128)(2,1)}), bf16[1024,512]{1,0:T(8,128)(2,1)}) %all-gather.5.cloned.1.call-update) | async-done | bytes 1048592 | tf_op jit(solution)/shard_map/all_gather | solution.py:72
  64.4 5.4 %collective-permute-start.1 = (bf16[1,1024,512]{2,1,0:T(8,128)(2,1)}, bf16[1,1024,512]{2,1,0:T(8,128)(2,1)S(1)}, u32[]{:S(2)}, u32[]{:S(2)}) collective-permute-start(bf16[1,1024,512]{2,1,0:T(8,128)(2,1)} %bitcast.144), channel_id=1, source_target_pairs={{8,0},{16,8},{24,16},{32,24},{40,32},{48,40},{56,48},{64,56},{72,6... | collective-permute-start | bytes 3145736 | tf_op jit(solution)/shard_map/ppermute | solution.py:15
  72.2 20.8 %collective-permute-done.1 = bf16[1,1024,512]{2,1,0:T(8,128)(2,1)S(1)} collective-permute-done((bf16[1,1024,512]{2,1,0:T(8,128)(2,1)}, bf16[1,1024,512]{2,1,0:T(8,128)(2,1)S(1)}, u32[]{:S(2)}, u32[]{:S(2)}) %collective-permute-start.1) | collective-permute-done | bytes 1048608 | tf_op jit(solution)/shard_map/ppermute | solution.py:15
  93.0 5.4 %collective-permute-done = bf16[1,1024,512]{2,1,0:T(8,128)(2,1)S(1)} collective-permute-done((bf16[1,1024,512]{2,1,0:T(8,128)(2,1)}, bf16[1,1024,512]{2,1,0:T(8,128)(2,1)S(1)}, u32[]{:S(2)}, u32[]{:S(2)}) %collective-permute-start) | collective-permute-done | bytes 1048608 | tf_op jit(solution)/shard_map/ppermute | solution.py:14
  98.4 5.1 %convolution_bitcast_fusion = f32[3,512,512]{1,2,0:T(8,128)} fusion(bf16[1,1024,512]{2,1,0:T(8,128)(2,1)S(1)} %collective-permute-done.1, bf16[1,1024,512]{2,1,0:T(8,128)(2,1)} %bitcast.146, bf16[1,1024,512]{2,1,0:T(8,128)(2,1)S(1)} %collective-permute-done, bf16[128,3,1024]{0,2,1:T(8,128)(2,1)S(1)} %bitcast.141, bf16[3,1024]{1,0:T(4,128)(2,1)S(1)} %bitcast.142, ...), kind=kOutput, calls=%fused_computation.21 | convolution fusion | flops 607715328 | bytes 7215104 | tf_op jit(solution)/shard_map/rt,jru->jtu/dot_general | solution.py:76
  104.3 2.6 broadcast_in_dim.12
  106.9 4.2 reshape.60
  111.0 58.8 %all-reduce.2.cloned.1.call-done = f32[3,512,512]{1,2,0:T(8,128)} async-done(((f32[3,512,512]{1,2,0:T(8,128)}), f32[3,512,512]{1,2,0:T(8,128)}) %all-reduce.2.cloned.1.call-update) | async-done | bytes 3145744 | tf_op jit(solution)/shard_map/psum | solution.py:84
  169.8 2.6 mul.94
  175.1 8.7 %gather_fusion = f32[512]{0:T(512)S(1)} fusion(f32[512,512]{0,1:T(8,128)} %slice_bitcast_fusion.42, s32[512]{0:T(512)S(1)} %bitcast.139), kind=kCustom, calls=%fused_computation | custom fusion | bytes 8192 | tf_op jit(solution)/shard_map/jit(diagonal)/cond/branch_0_fun/gather | solution.py:85
  185.7 75.6 %pmax.7 = f32[]{:T(128)} all-reduce(f32[]{:T(128)} %reduce_max.9), channel_id=1, replica_groups=mesh['space'=32,'grp'=8] {'space'}, use_global_device_ids=true, to_apply=%region_2.3 | all-reduce | flops 1 | bytes 8 | tf_op jit(solution)/shard_map/pmax | solution.py:85
  261.4 4.1 fusion.1
  266.2 2.2 collective-permute-start.2
  272.2 1.9 fusion.46
  274.1 27.2 %collective-permute-done.3 = f32[2,512,512]{1,2,0:T(8,128)S(1)} collective-permute-done((f32[2,512,512]{1,2,0:T(8,128)S(1)}, f32[2,512,512]{1,2,0:T(8,128)S(1)}, u32[]{:S(2)}, u32[]{:S(2)}) %collective-permute-start.3) | collective-permute-done | bytes 2097184 | tf_op jit(solution)/shard_map/ppermute | solution.py:15
  301.3 1.9 fusion.27
  305.1 1.9 fusion.30
  307.0 12.4 %fusion.29 = f32[1,512,512]{1,2,0:T(8,128)S(1)} fusion(f32[512,512]{0,1:T(8,128)S(1)} %fusion.44, f32[512,512]{0,1:T(8,128)S(1)} %fusion.50, f32[2,512,512]{1,2,0:T(8,128)S(1)} %collective-permute-done.2, f32[3,512,512]{1,2,0:T(8,128)S(1)} %get-tuple-element.5), kind=kOutput, calls=%fused_computation.43 | convolution fusion | flops 1611137024 | bytes 5242880 | tf_op jit(solution)/shard_map/dot_general | solution.py:21
  320.7 3.7 collective-permute-start.5
  330.0 26.4 %collective-permute-done.5 = f32[2,512,512]{1,2,0:T(8,128)S(1)} collective-permute-done((f32[2,512,512]{1,2,0:T(8,128)S(1)}, f32[2,512,512]{1,2,0:T(8,128)S(1)}, u32[]{:S(2)}, u32[]{:S(2)}) %collective-permute-start.5) | collective-permute-done | bytes 2097184 | tf_op jit(solution)/shard_map/ppermute | solution.py:15
  356.4 1.9 fusion.23
  358.3 1.9 fusion.41
  363.8 2.1 fusion.25
  367.2 4.1 collective-permute-start.7
  377.0 25.4 %collective-permute-done.7 = f32[2,512,512]{1,2,0:T(8,128)S(1)} collective-permute-done((f32[2,512,512]{1,2,0:T(8,128)S(1)}, f32[2,512,512]{1,2,0:T(8,128)S(1)}, u32[]{:S(2)}, u32[]{:S(2)}) %collective-permute-start.7) | collective-permute-done | bytes 2097184 | tf_op jit(solution)/shard_map/ppermute | solution.py:15
  402.5 1.9 fusion.19
  404.3 1.9 fusion.37
  409.9 1.9 fusion.21
  411.8 2.8 fusion.10
  414.5 2.3 copy.56
  (53 shorter events, 38.3 us)
Async XLA Ops:
  6.5 29.6 %all-gather.3.cloned.1.call-start = ((), (), s32[]{:S(2)}) async-start(), calls=%async_computation | async-start | bytes 1179648 | tf_op jit(solution)/shard_map/all_gather | solution.py:65
  8.9 55.5 %all-gather.5.cloned.1.call-start = ((), (), s32[]{:S(2)}) async-start(), calls=%async_computation.1 | async-start | bytes 1179648 | tf_op jit(solution)/shard_map/all_gather | solution.py:72
  38.5 131.3 %all-reduce.2.cloned.1.call-start = ((), (), s32[]{:S(2)}) async-start(), calls=%async_computation.2 | async-start | bytes 6291456 | tf_op jit(solution)/shard_map/psum | solution.py:84
  64.4 28.6 %collective-permute-start.1 = (bf16[1,1024,512]{2,1,0:T(8,128)(2,1)}, bf16[1,1024,512]{2,1,0:T(8,128)(2,1)S(1)}, u32[]{:S(2)}, u32[]{:S(2)}) collective-permute-start(bf16[1,1024,512]{2,1,0:T(8,128)(2,1)} %bitcast.144), channel_id=1, source_target_pairs={{8,0},{16,8},{24,16},{32,24},{40,32},{48,40},{56,48},{64,56},{72,6... | collective-permute-start | bytes 3145736 | tf_op jit(solution)/shard_map/ppermute | solution.py:15
  69.9 28.5 %collective-permute-start = (bf16[1,1024,512]{2,1,0:T(8,128)(2,1)}, bf16[1,1024,512]{2,1,0:T(8,128)(2,1)S(1)}, u32[]{:S(2)}, u32[]{:S(2)}) collective-permute-start(bf16[1,1024,512]{2,1,0:T(8,128)(2,1)} %bitcast.145), channel_id=1, source_target_pairs={{0,8},{8,16},{16,24},{24,32},{32,40},{40,48},{48,56},{56,64},{64,7... | collective-permute-start | bytes 3145736 | tf_op jit(solution)/shard_map/ppermute | solution.py:14
  103.5 0.7 copy-start.2
  172.4 1.6 copy-start
  266.1 35.2 %collective-permute-start.3 = (f32[2,512,512]{1,2,0:T(8,128)S(1)}, f32[2,512,512]{1,2,0:T(8,128)S(1)}, u32[]{:S(2)}, u32[]{:S(2)}) collective-permute-start(f32[2,512,512]{1,2,0:T(8,128)S(1)} %get-tuple-element.12), channel_id=1, source_target_pairs={{8,0},{16,8},{24,16},{32,24},{40,32},{48,40},{56,48},{64,56},{72,6... | collective-permute-start | bytes 6291464 | tf_op jit(solution)/shard_map/ppermute | solution.py:15
  266.2 38.9 %collective-permute-start.2 = (f32[2,512,512]{1,2,0:T(8,128)S(1)}, f32[2,512,512]{1,2,0:T(8,128)S(1)}, u32[]{:S(2)}, u32[]{:S(2)}) collective-permute-start(f32[2,512,512]{1,2,0:T(8,128)S(1)} %get-tuple-element.11), channel_id=1, source_target_pairs={{0,8},{8,16},{16,24},{24,32},{32,40},{40,48},{48,56},{56,64},{64,7... | collective-permute-start | bytes 6291464 | tf_op jit(solution)/shard_map/ppermute | solution.py:14
  320.7 35.7 %collective-permute-start.5 = (f32[2,512,512]{1,2,0:T(8,128)S(1)}, f32[2,512,512]{1,2,0:T(8,128)S(1)}, u32[]{:S(2)}, u32[]{:S(2)}) collective-permute-start(f32[2,512,512]{1,2,0:T(8,128)S(1)} %get-tuple-element.10), channel_id=1, source_target_pairs={{8,0},{16,8},{24,16},{32,24},{40,32},{48,40},{56,48},{64,56},{72,6... | collective-permute-start | bytes 6291464 | tf_op jit(solution)/shard_map/ppermute | solution.py:15
  324.4 37.5 %collective-permute-start.4 = (f32[2,512,512]{1,2,0:T(8,128)S(1)}, f32[2,512,512]{1,2,0:T(8,128)S(1)}, u32[]{:S(2)}, u32[]{:S(2)}) collective-permute-start(f32[2,512,512]{1,2,0:T(8,128)S(1)} %get-tuple-element.9), channel_id=1, source_target_pairs={{0,8},{8,16},{16,24},{24,32},{32,40},{40,48},{48,56},{56,64},{64,7... | collective-permute-start | bytes 6291464 | tf_op jit(solution)/shard_map/ppermute | solution.py:14
  367.2 35.2 %collective-permute-start.7 = (f32[2,512,512]{1,2,0:T(8,128)S(1)}, f32[2,512,512]{1,2,0:T(8,128)S(1)}, u32[]{:S(2)}, u32[]{:S(2)}) collective-permute-start(f32[2,512,512]{1,2,0:T(8,128)S(1)} %get-tuple-element.8), channel_id=1, source_target_pairs={{8,0},{16,8},{24,16},{32,24},{40,32},{48,40},{56,48},{64,56},{72,6... | collective-permute-start | bytes 6291464 | tf_op jit(solution)/shard_map/ppermute | solution.py:15
  371.4 36.6 %collective-permute-start.6 = (f32[2,512,512]{1,2,0:T(8,128)S(1)}, f32[2,512,512]{1,2,0:T(8,128)S(1)}, u32[]{:S(2)}, u32[]{:S(2)}) collective-permute-start(f32[2,512,512]{1,2,0:T(8,128)S(1)} %get-tuple-element.7), channel_id=1, source_target_pairs={{0,8},{8,16},{16,24},{24,32},{32,40},{40,48},{48,56},{56,64},{64,7... | collective-permute-start | bytes 6291464 | tf_op jit(solution)/shard_map/ppermute | solution.py:14
  409.9 1.9 copy-start.1
Sparse Core Ops, SparseCore 0:
  9.2 26.8 all-gather.2
  38.6 25.7 all-gather.4
  103.6 66.1 all-reduce.1
where the time goes:
time: 432 us; the launch traced here: 424 us
  waiting for transfers between devices  220 us (51%)
  blocking collectives  75.6 us (17%)
  matrix products  60.2 us (14%)
  local copies, waits for them, and re-layouts  24.9 us (6%)
  starting transfers between devices  15.7 us (4%)
  between operations  13.8 us (3%)
  other arithmetic  13.6 us (3%)
    ppermute x4, waiting for transfers between devices, padded(): after = lax.ppermute(leading, axis, down)  99.8 us
    pmax x1, blocking collectives, per_device(): peak = lax.pmax(jnp.max(jnp.diagonal(blocks[1])), 'space')  75.6 us
    psum x1, waiting for transfers between devices, per_device(): blocks = lax.psum(partial_sums, 'grp') * pair_mask  58.8 us
    dot_general x21, matrix products, matmul_high(): jnp.dot(left_side, right_side, precision=lax.Precision.HIGHEST, preferred...  50 us
    all_gather x1, waiting for transfers between devices, per_device(): lax.all_gather(trial_eff, 'grp', axis=0, tiled=True)  26.5 us
    all_gather x1, waiting for transfers between devices, per_device(): domain_psi = lax.all_gather(projected, 'grp', axis=0, tiled=True)  25.9 us
    ppermute x4, starting transfers between devices, padded(): after = lax.ppermute(leading, axis, down)  13.3 us
    ppermute x4, waiting for transfers between devices, padded(): before = lax.ppermute(last, axis, up)  8.94 us
  transfers between devices with their start and end apart: 11, of which 10 were waited for; matrix products, arithmetic and copies ran while one was open for 9% of the time, Pallas kernels for 0%

commit v1 on v0

v1 whole, which is shorter than its diff:
```python
import jax
import jax.numpy as jnp
from jax import lax
from jax.experimental import pallas as pl
from jax.experimental.pallas import tpu as pltpu
from jax.sharding import PartitionSpec as P

BF = jnp.bfloat16
F32 = jnp.float32
ATOM = 128
WIDTH = 256
COLS = 512
ROWS = 1024
CHIP_ROWS = 256
LEVELS = 4
HIGH = 48 * 1024 * 1024


def here():
    grp = lax.axis_index("grp")
    return grp // 2, lax.rem(grp, 2)


def dot(left, right):
    return jnp.dot(left, right, preferred_element_type=F32)


def keep_if(flag, block):
    return jnp.where(flag != 0, block, jnp.zeros_like(block))


def smem():
    return pl.BlockSpec(memory_space=pltpu.SMEM)


def vmem():
    return pl.BlockSpec(memory_space=pltpu.VMEM)


def call(body, outs, ins, specs, scratch=(), flops=0):
    size = sum(x.size * x.dtype.itemsize for x in ins) + sum(
        o.size * o.dtype.itemsize for o in outs
    )
    return pl.pallas_call(
        body,
        out_shape=outs,
        in_specs=specs,
        out_specs=[vmem() for _ in outs],
        scratch_shapes=list(scratch),
        compiler_params=pltpu.CompilerParams(vmem_limit_bytes=HIGH),
        cost_estimate=pl.CostEstimate(flops=flops, bytes_accessed=size, transcendentals=0),
    )(*ins)


def shape(rows, cols, dtype=BF):
    return jax.ShapeDtypeStruct((rows, cols), dtype)


def shift(array, axis, by):
    n = lax.axis_size(axis)
    return lax.ppermute(array, axis, [(i, (i + by) % n) for i in range(n)])


def swap_core(array):
    n = lax.axis_size("grp")
    return lax.ppermute(array, "grp", [(i, i ^ 1) for i in range(n)])


def along_y(array):
    return [shift(array, "grp", -2), shift(array, "grp", 4), shift(array, "grp", 2)]


def mask_trial(support, trial, out):
    for t in range(2):
        cols = slice(t * WIDTH, (t + 1) * WIDTH)
        out[:, cols] = keep_if(support[0, t], trial[:, cols])


def mask_rows(dens_pat, marg_pat, dens, marg, dens_own, dens_pair, marg_out):
    y, core = here()
    for k in range(LEVELS):
        for side, target in ((core, dens_own), (1 - core, dens_pair)):
            block = lax.rem(y + k, LEVELS) * 2 + side
            start = pl.multiple_of(block * ATOM, ATOM)
            target[:, k * ATOM : (k + 1) * ATOM] = keep_if(
                dens_pat[0, block], dens[:, pl.ds(start, ATOM)]
            )
    for b in range(16):
        cols = slice(b * ATOM, (b + 1) * ATOM)
        marg_out[:, cols] = keep_if(marg_pat[0, b], marg[:, cols])


def project(dens_own, dens_pair, t0, t1, t2, t3, kept, sent):
    y, core = here()
    stacked = jnp.concatenate([t0[...], t1[...], t2[...], t3[...]], axis=0)
    for dens, rows in ((dens_own, core), (dens_pair, 1 - core)):
        part = dot(dens[...], stacked)
        low, high = part[:, :WIDTH], part[:, WIDTH:]
        at = pl.ds(pl.multiple_of(rows * ATOM, ATOM), ATOM)
        kept[at, :] = jnp.where(core == 0, low, high)
        sent[at, :] = jnp.where(core == 0, high, low)


def gram(
    pair, p0, p1, p2, p3, q0, q1, q2, q3, other, m_own, m_pair,
    kept, s1, s2, s3, rows_out, own, near, left, marg,
):
    y, core = here()
    for k, (p, q) in enumerate(((p0, q0), (p1, q1), (p2, q2), (p3, q3))):
        at = pl.ds(pl.multiple_of(lax.rem(y + k, LEVELS) * CHIP_ROWS, CHIP_ROWS), CHIP_ROWS)
        own[at, :] = p[...]
        near[at, :] = q[...]
    left[:, pl.ds(pl.multiple_of(core * WIDTH, WIDTH), WIDTH)] = p0[...]
    left[:, pl.ds(pl.multiple_of((1 - core) * WIDTH, WIDTH), WIDTH)] = other[...]
    marg[pl.ds(pl.multiple_of(core * ATOM, ATOM), ATOM), :] = m_own[...]
    marg[pl.ds(pl.multiple_of((1 - core) * ATOM, ATOM), ATOM), :] = m_pair[...]
    rows_out[...] = left[pl.ds(pl.multiple_of(core * ATOM, ATOM), ATOM), :]
    applied_own = dot(marg[:, ROWS:], own[...]).astype(BF)
    applied_near = dot(marg[:, :ROWS], near[...]).astype(BF)
    diag = jnp.sum(p0[...].astype(F32) * applied_own.astype(F32), axis=0, keepdims=True)
    high = diag.astype(BF).astype(F32)
    row = lax.broadcasted_iota(jnp.int32, (16, WIDTH), 0)
    tail = jnp.where(row == 0, high, jnp.where(row == 1, diag - high, 0.0))
    for k, out in enumerate((kept, s1, s2, s3)):
        chunk = lax.rem(y + k, LEVELS)
        lanes = pl.ds(pl.multiple_of(chunk * ATOM, ATOM), ATOM)
        rows = left[:, lanes].T
        own_flag = pair[0, 1, chunk // 2, core]
        near_flag = pair[0, 0, chunk // 2, core]
        out[:ATOM, :] = keep_if(own_flag, dot(rows, applied_own)).astype(out.dtype)
        out[ATOM : 2 * ATOM, :] = keep_if(near_flag, dot(rows, applied_near)).astype(out.dtype)
        out[2 * ATOM :, :] = tail.astype(out.dtype)


def add_parts(kept, s1, s2, s3, shard, own_out, peak):
    total = kept[...]
    for s in (s1, s2, s3):
        total = total + s[...].astype(F32)
    shard[...] = total[: 2 * ATOM].astype(BF)
    own_out[...] = total[:ATOM].astype(BF)
    diag = jnp.sum(total[2 * ATOM :], axis=0, keepdims=True)
    peak[...] = jnp.full((8, 128), jnp.max(diag), F32)


def purify(
    pair, peak, own_mine, own_pair, near_mine, near_pair, row_before, row_here, row_after,
    to_before, here_out, to_after, band, power, total,
):
    y, core = here()
    level = jnp.max(peak[...])
    ones = jnp.full((8, 128), level, F32)
    scale = jnp.max(jnp.exp2(-jnp.floor(jnp.log2(jnp.abs(ones)))))
    inverse = jnp.max(1.0 / (ones * scale))

    def place(row, col, block, side, k):
        chunk = lax.rem(y + k, LEVELS)
        at = pl.ds(pl.multiple_of(row * COLS + chunk * ATOM, ATOM), ATOM)
        lanes = pl.ds(pl.multiple_of(col * COLS + side * WIDTH, WIDTH), WIDTH)
        band[at, lanes] = (block.astype(F32) * scale).astype(BF)

    for own, near, side in ((own_mine, near_mine, core), (own_pair, near_pair, 1 - core)):
        for k in range(LEVELS):
            base = k * 2 * ATOM
            place(1, 1, own[base : base + ATOM, :], side, k)
            place(1, 0, own[base + ATOM : base + 2 * ATOM, :], side, k)
            base = k * 3 * ATOM
            place(0, 0, near[base : base + ATOM, :], side, k)
            place(2, 2, near[base + ATOM : base + 2 * ATOM, :], side, k)
            place(2, 1, near[base + 2 * ATOM : base + 3 * ATOM, :], side, k)
    band[:COLS, COLS : 2 * COLS] = band[COLS : 2 * COLS, :COLS].T
    band[COLS : 2 * COLS, 2 * COLS :] = band[2 * COLS :, COLS : 2 * COLS].T

    row = lax.broadcasted_iota(jnp.int32, (ATOM, ATOM), 0)
    col = lax.broadcasted_iota(jnp.int32, (ATOM, ATOM), 1)
    on_diag = row == col
    gathered = jnp.zeros((ATOM, ATOM), F32)
    for b in range(LEVELS):
        at = slice(COLS + b * ATOM, COLS + (b + 1) * ATOM)
        gathered = gathered + jnp.where(on_diag, band[at, at].astype(F32), 0.0)
    mean = jnp.full((16, 128), jnp.sum(gathered) * (1.0 / COLS), F32)
    centre = jnp.max(mean.astype(BF).astype(F32))
    for b in range(3 * LEVELS):
        at = slice(b * ATOM, (b + 1) * ATOM)
        block = band[at, at].astype(F32)
        band[at, at] = jnp.where(on_diag, block - centre, block).astype(BF)

    c = inverse
    x = centre * c
    g0 = 2.25 + x * (-2.4375 + x * (1.6875 + x * (-0.5625 + x * 0.0625)))
    g1 = (-2.4375 + x * (3.375 + x * (-1.6875 + x * 0.25))) * c
    g2 = (1.6875 + x * (-1.6875 + x * 0.375)) * c * c
    g3 = (-0.5625 + x * 0.25) * c * c * c
    g4 = 0.0625 * c * c * c * c

    power[0] = band[:, COLS : 2 * COLS]
    total[...] = g1 * power[0].astype(F32)

    def step(n, carry):
        gain = jnp.where(n == 0, g2, jnp.where(n == 1, g3, g4))
        source = lax.rem(n, 2)
        for r in range(3):
            first, last = max(r - 1, 0) * COLS, min(r + 2, 3) * COLS
            product = dot(band[r * COLS : (r + 1) * COLS, first:last], power[source, first:last, :])
            for t in range(2):
                for u in range(2):
                    flag = pair[0, 1, t, u] if r == 1 else pair[0, r, u, t]
                    part = keep_if(
                        flag,
                        product[t * WIDTH : (t + 1) * WIDTH, u * WIDTH : (u + 1) * WIDTH],
                    )
                    at = slice(r * COLS + t * WIDTH, r * COLS + (t + 1) * WIDTH)
                    lanes = slice(u * WIDTH, (u + 1) * WIDTH)
                    power[1 - source, at, lanes] = part.astype(BF)
                    total[at, lanes] += gain * part
        return carry

    lax.fori_loop(0, 3, step, 0)
    to_before[...] = dot(row_before[...], total[:COLS].astype(BF)).astype(BF)
    here_out[...] = g0 * row_here[...].astype(F32) + dot(
        row_here[...], total[COLS : 2 * COLS].astype(BF)
    )
    to_after[...] = dot(row_after[...], total[2 * COLS :].astype(BF)).astype(BF)


def assemble(before, own, after, out):
    out[:, :COLS] = before[...].astype(F32)
    out[:, COLS : 2 * COLS] = own[...]
    out[:, 2 * COLS :] = after[...].astype(F32)


def per_device(trial, support, density, density_pattern, margin, margin_pattern, pair_pattern):
    (slab,) = call(mask_trial, [shape(ATOM, COLS)], [support, trial], [smem(), vmem()])
    slabs = along_y(slab)
    dens_own, dens_pair, marg = pl.pallas_call(
        mask_rows,
        out_shape=[shape(ATOM, COLS), shape(ATOM, COLS), shape(ATOM, 2 * ROWS)],
        grid=(1,),
        in_specs=[
            smem(),
            smem(),
            pl.BlockSpec((ATOM, ROWS), lambda i: (0, 0)),
            pl.BlockSpec((ATOM, 2 * ROWS), lambda i: (0, 0)),
        ],
        out_specs=[
            pl.BlockSpec((ATOM, COLS), lambda i: (0, 0)),
            pl.BlockSpec((ATOM, COLS), lambda i: (0, 0)),
            pl.BlockSpec((ATOM, 2 * ROWS), lambda i: (0, 0)),
        ],
        compiler_params=pltpu.CompilerParams(vmem_limit_bytes=HIGH),
        cost_estimate=pl.CostEstimate(flops=0, bytes_accessed=2 * 2**20, transcendentals=0),
    )(density_pattern, margin_pattern, density, margin)
    dens_got = swap_core(dens_pair)
    marg_got = swap_core(marg)
    kept, sent = call(
        project,
        [shape(CHIP_ROWS, WIDTH, F32), shape(CHIP_ROWS, WIDTH, F32)],
        [dens_own, dens_got, slab, *slabs],
        [vmem()] * 6,
        flops=2 * 256 * 512 * 512,
    )
    projected = (kept + swap_core(sent)).astype(BF)
    near = shift(projected, "space", 1)
    own_pieces = along_y(projected)
    other = swap_core(projected)
    near_pieces = along_y(near)
    tail = 2 * ATOM + 16
    kept, s1, s2, s3, rows_here = call(
        gram,
        [shape(tail, WIDTH, F32)] + [shape(tail, WIDTH)] * 3 + [shape(ATOM, COLS)],
        [pair_pattern, projected, *own_pieces, near, *near_pieces, other, marg, marg_got],
        [smem()] + [vmem()] * 11,
        scratch=[
            pltpu.VMEM((ROWS, WIDTH), BF),
            pltpu.VMEM((ROWS, WIDTH), BF),
            pltpu.VMEM((CHIP_ROWS, COLS), BF),
            pltpu.VMEM((CHIP_ROWS, 2 * ROWS), BF),
        ],
        flops=2 * 256 * 256 * (2048 + 1024),
    )
    got = [shift(s1, "grp", 2), shift(s2, "grp", 4), shift(s3, "grp", -2)]
    shard, own_shard, peak = call(
        add_parts,
        [shape(2 * ATOM, WIDTH), shape(ATOM, WIDTH), shape(8, 128, F32)],
        [kept, *got],
        [vmem()] * 4,
    )
    below = shift(own_shard, "space", 1)
    above = shift(shard, "space", -1)
    own_band = jnp.concatenate([shard, *along_y(shard)], axis=0)
    own_band_pair = swap_core(own_band)
    near_shard = jnp.concatenate([below, above], axis=0)
    near_band = jnp.concatenate([near_shard, *along_y(near_shard)], axis=0)
    near_band_pair = swap_core(near_band)
    peak = jnp.maximum(peak, swap_core(peak))
    for by in (1, 3, 9):
        peak = jnp.maximum(
            peak, jnp.maximum(shift(peak, "space", by), shift(peak, "space", -by))
        )
    peak = jnp.maximum(peak, shift(peak, "space", 5))
    rows_before = shift(rows_here, "space", 1)
    rows_after = shift(rows_here, "space", -1)
    to_before, result, to_after = call(
        purify,
        [shape(ATOM, COLS), shape(ATOM, COLS, F32), shape(ATOM, COLS)],
        [
            pair_pattern, peak, own_band, own_band_pair, near_band, near_band_pair,
            rows_before, rows_here, rows_after,
        ],
        [smem()] + [vmem()] * 8,
        scratch=[
            pltpu.VMEM((3 * COLS, 3 * COLS), BF),
            pltpu.VMEM((2, 3 * COLS, COLS), BF),
            pltpu.VMEM((3 * COLS, COLS), F32),
        ],
        flops=2 * 21 * 512**3,
    )
    before = shift(to_after, "space", 1)
    after = shift(to_before, "space", -1)
    (out,) = call(
        assemble, [shape(ATOM, 3 * COLS, F32)], [before, result, after], [vmem()] * 3
    )
    return out


def solution(mesh):
    placed = (
        P(("space", "grp"), None),
        P(("space", "grp"), None),
        P(("space", "grp"), None),
        P(("space", "grp"), None),
        P(("space", "grp"), None),
        P(("space", "grp"), None),
        P("space", None, None, None),
    )
    return jax.shard_map(
        per_device, mesh=mesh, in_specs=placed, out_specs=P(("space", "grp"), None), check_vma=False
    )
```

time: 432 us -> 132 us (0.31); the launches traced: 424 us -> 132 us
  waiting for transfers between devices: 220 us -> 55.4 us
  blocking collectives: 75.6 us -> 0 us
  matrix products: 60.2 us -> 0 us
  starting transfers between devices: 15.7 us -> 58.1 us
  local copies, waits for them, and re-layouts: 24.9 us -> 3.61 us
  Pallas kernels: 0 us -> 14.4 us
  other arithmetic: 13.6 us -> 0.05 us
  between operations: 13.8 us -> 0.26 us
    pmax x1 -> x0, blocking collectives: 75.6 us -> none  [per_device(): peak = lax.pmax(jnp.max(jnp.diagonal(blocks[1])), 'space')]
    dot_general x24 -> x0, matrix products: 60.2 us -> none  [the longest x21 50 us: matmul_high(): jnp.dot(left_side, right_side, precision=lax.Precision.HIGHEST, preferred...]
    psum x1 -> x0, waiting for transfers between devices: 58.8 us -> none  [per_device(): blocks = lax.psum(partial_sums, 'grp') * pair_mask]
    ppermute x8 -> x39, waiting for transfers between devices: 109 us -> 55.4 us  [the longest x32 54.4 us: shift(): return lax.ppermute(array, axis, [(i, (i + by) % n) for i in range(n)])]
    all_gather x2 -> x0, waiting for transfers between devices: 52.4 us -> none  [the longest x1 26.5 us: per_device(): lax.all_gather(trial_eff, 'grp', axis=0, tiled=True)]
    ppermute x8 -> x39, starting transfers between devices: 15.6 us -> 58.1 us  [the longest x32 56.8 us: shift(): return lax.ppermute(array, axis, [(i, (i + by) % n) for i in range(n)])]
    pallas_call x0 -> x7, Pallas kernels: none -> 14.4 us  [the longest x6 13.6 us: call(): pl.pallas_call(body, out_shape=outs, in_specs=specs, out_specs=[vmem() fo...]
    mul x7 -> x0, other arithmetic: 11.1 us -> none  [the longest x1 4.09 us: per_device(): z_one = pair_mask * (1.5 * identity_band - 0.5 * scaled)]
  transfers between devices with their start and end apart: 11 -> 39, of which waited for: 10 -> 18; matrix products, arithmetic and copies ran while one was open for 9% -> 0% of each run, Pallas kernels for 0% -> 1%
where the time goes in v1:
time: 132 us
  starting transfers between devices  58.1 us (44%)
  waiting for transfers between devices  55.4 us (42%)
  Pallas kernels  14.4 us (11%)
  local copies, waits for them, and re-layouts  3.61 us (3%)
    ppermute x32, starting transfers between devices, shift(): return lax.ppermute(array, axis, [(i, (i + by) % n) for i in range(n)])  56.8 us
    ppermute x32, waiting for transfers between devices, shift(): return lax.ppermute(array, axis, [(i, (i + by) % n) for i in range(n)])  54.4 us
    pallas_call x6, Pallas kernels, call(): pl.pallas_call(body, out_shape=outs, in_specs=specs, out_specs=[vmem() fo...  13.6 us
    unnamed x21, local copies, waits for them, and re-layouts  3.57 us
  transfers between devices with their start and end apart: 39, of which 18 were waited for; matrix products, arithmetic and copies ran while one was open for 0% of the time, Pallas kernels for 1%

profile of v1, /device:TPU:24, one launch (start us, length us, event | category | flops | bytes accessed | tf_op | source)
XLA Modules:
  0.0 131.9 jit_solution(11233419250436538510)
XLA Ops:
  3.0 2.7 %collective-permute-start.2 = (bf16[128,512]{1,0:T(8,128)(2,1)S(1)}, bf16[128,512]{1,0:T(8,128)(2,1)S(1)}, u32[]{:S(2)}, u32[]{:S(2)}) collective-permute-start(bf16[128,512]{1,0:T(8,128)(2,1)S(1)} %shard_map.74.t0), channel_id=1, source_target_pairs={{0,4},{1,5},{2,6},{3,7},{4,0},{5,1},{6,2},{7,3},{8,12},{9,13},{10,... | collective-permute-start | bytes 393224 | tf_op jit(solution)/shard_map/ppermute | solution.py:61
  6.1 1.1 copy-done
  8.8 2.7 %collective-permute-done.1.t1 = bf16[128,512]{1,0:T(8,128)(2,1)S(1)} collective-permute-done((bf16[128,512]{1,0:T(8,128)(2,1)S(1)}, bf16[128,512]{1,0:T(8,128)(2,1)S(1)}, u32[]{:S(2)}, u32[]{:S(2)}) %collective-permute-start.1) | collective-permute-done | bytes 131104 | tf_op jit(solution)/shard_map/ppermute | solution.py:61
  13.0 1.0 collective-permute-done.4
  14.1 2.0 %collective-permute-start.8 = (bf16[256,256]{1,0:T(8,128)(2,1)S(1)}, bf16[256,256]{1,0:T(8,128)(2,1)S(1)}, u32[]{:S(2)}, u32[]{:S(2)}) collective-permute-start(bf16[256,256]{1,0:T(8,128)(2,1)S(1)} %add_convert_fusion.p0), channel_id=1, source_target_pairs={{0,8},{8,16},{16,24},{24,32},{32,40},{40,48},{48,56},{56,64},{64,7... | collective-permute-start | bytes 393224 | tf_op jit(solution)/shard_map/ppermute | solution.py:61
  16.7 3.5 %collective-permute-start.6 = (bf16[256,256]{1,0:T(8,128)(2,1)S(1)}, bf16[256,256]{1,0:T(8,128)(2,1)S(1)}, u32[]{:S(2)}, u32[]{:S(2)}) collective-permute-start(bf16[256,256]{1,0:T(8,128)(2,1)S(1)} %add_convert_fusion.p0), channel_id=1, source_target_pairs={{0,4},{1,5},{2,6},{3,7},{4,0},{5,1},{6,2},{7,3},{8,12},{9,13},{10,... | collective-permute-start | bytes 393224 | tf_op jit(solution)/shard_map/ppermute | solution.py:61
  20.2 5.8 %collective-permute-done.8.q0 = bf16[256,256]{1,0:T(8,128)(2,1)S(1)} collective-permute-done((bf16[256,256]{1,0:T(8,128)(2,1)S(1)}, bf16[256,256]{1,0:T(8,128)(2,1)S(1)}, u32[]{:S(2)}, u32[]{:S(2)}) %collective-permute-start.8) | collective-permute-done | bytes 131104 | tf_op jit(solution)/shard_map/ppermute | solution.py:61
  26.0 2.7 %collective-permute-start.7 = (bf16[256,256]{1,0:T(8,128)(2,1)S(1)}, bf16[256,256]{1,0:T(8,128)(2,1)S(1)}, u32[]{:S(2)}, u32[]{:S(2)}) collective-permute-start(bf16[256,256]{1,0:T(8,128)(2,1)S(1)} %add_convert_fusion.p0), channel_id=1, source_target_pairs={{0,2},{1,3},{2,4},{3,5},{4,6},{5,7},{6,0},{7,1},{8,10},{9,11},{10,... | collective-permute-start | bytes 393224 | tf_op jit(solution)/shard_map/ppermute | solution.py:61
  28.7 2.0 %collective-permute-start.11 = (bf16[256,256]{1,0:T(8,128)(2,1)S(1)}, bf16[256,256]{1,0:T(8,128)(2,1)S(1)}, u32[]{:S(2)}, u32[]{:S(2)}) collective-permute-start(bf16[256,256]{1,0:T(8,128)(2,1)S(1)} %collective-permute-done.8.q0), channel_id=1, source_target_pairs={{0,2},{1,3},{2,4},{3,5},{4,6},{5,7},{6,0},{7,1},{8,10},{9,11},{10,... | collective-permute-start | bytes 393224 | tf_op jit(solution)/shard_map/ppermute | solution.py:61
  30.9 3.9 %collective-permute-done.7.p3 = bf16[256,256]{1,0:T(8,128)(2,1)S(1)} collective-permute-done((bf16[256,256]{1,0:T(8,128)(2,1)S(1)}, bf16[256,256]{1,0:T(8,128)(2,1)S(1)}, u32[]{:S(2)}, u32[]{:S(2)}) %collective-permute-start.7) | collective-permute-done | bytes 131104 | tf_op jit(solution)/shard_map/ppermute | solution.py:61
  34.7 1.7 %collective-permute-done.10.q2 = bf16[256,256]{1,0:T(8,128)(2,1)S(1)} collective-permute-done((bf16[256,256]{1,0:T(8,128)(2,1)S(1)}, bf16[256,256]{1,0:T(8,128)(2,1)S(1)}, u32[]{:S(2)}, u32[]{:S(2)}) %collective-permute-start.10) | collective-permute-done | bytes 131104 | tf_op jit(solution)/shard_map/ppermute | solution.py:61
  37.7 1.5 %shard_map.76 = (f32[272,256]{1,0:T(8,128)S(1)}, bf16[272,256]{1,0:T(8,128)(2,1)S(1)}, bf16[272,256]{1,0:T(8,128)(2,1)S(1)}, bf16[272,256]{1,0:T(8,128)(2,1)S(1)}, bf16[128,512]{1,0:T(8,128)(2,1)S(1)}) custom-call(s32[1,3,2,2]{3,2,1,0:T(2,128)S(1)} %copy.9.pair, bf16[256,256]{1,0:T(8,128)(2,1)S(1)} %add_convert_fusion.p0, ...), custom_call_target="tpu_custom_call" | custom-call | flops 402653184 | bytes 3055664 | tf_op jit(solution)/shard_map/pallas_call | solution.py:44
  39.2 2.9 %collective-permute-start.14 = (bf16[272,256]{1,0:T(8,128)(2,1)S(1)}, bf16[272,256]{1,0:T(8,128)(2,1)S(1)}, u32[]{:S(2)}, u32[]{:S(2)}) collective-permute-start(bf16[272,256]{1,0:T(8,128)(2,1)S(1)} %get-tuple-element.27), channel_id=1, source_target_pairs={{0,2},{1,3},{2,4},{3,5},{4,6},{5,7},{6,0},{7,1},{8,10},{9,11},{10,... | collective-permute-start | bytes 417800 | tf_op jit(solution)/shard_map/ppermute | solution.py:61
  43.1 4.4 %collective-permute-done.14.s1 = bf16[272,256]{1,0:T(8,128)(2,1)S(1)} collective-permute-done((bf16[272,256]{1,0:T(8,128)(2,1)S(1)}, bf16[272,256]{1,0:T(8,128)(2,1)S(1)}, u32[]{:S(2)}, u32[]{:S(2)}) %collective-permute-start.14) | collective-permute-done | bytes 139296 | tf_op jit(solution)/shard_map/ppermute | solution.py:61
  47.5 2.3 %collective-permute-done.15.s2 = bf16[272,256]{1,0:T(8,128)(2,1)S(1)} collective-permute-done((bf16[272,256]{1,0:T(8,128)(2,1)S(1)}, bf16[272,256]{1,0:T(8,128)(2,1)S(1)}, u32[]{:S(2)}, u32[]{:S(2)}) %collective-permute-start.15) | collective-permute-done | bytes 139296 | tf_op jit(solution)/shard_map/ppermute | solution.py:61
  49.8 1.1 collective-permute-done.16.s3
  51.2 5.3 %collective-permute-start.30 = (bf16[256,256]{1,0:T(8,128)(2,1)S(1)}, bf16[256,256]{1,0:T(8,128)(2,1)S(1)}, u32[]{:S(2)}, u32[]{:S(2)}) collective-permute-start(bf16[256,256]{1,0:T(8,128)(2,1)S(1)} %get-tuple-element.31), channel_id=1, source_target_pairs={{0,248},{8,0},{16,8},{24,16},{32,24},{40,32},{48,40},{56,48},{64,5... | collective-permute-start | bytes 393224 | tf_op jit(solution)/shard_map/ppermute | solution.py:61
  56.6 2.3 %collective-permute-start.26 = (bf16[256,256]{1,0:T(8,128)(2,1)S(1)}, bf16[256,256]{1,0:T(8,128)(2,1)S(1)}, u32[]{:S(2)}, u32[]{:S(2)}) collective-permute-start(bf16[256,256]{1,0:T(8,128)(2,1)S(1)} %get-tuple-element.31), channel_id=1, source_target_pairs={{0,4},{1,5},{2,6},{3,7},{4,0},{5,1},{6,2},{7,3},{8,12},{9,13},{10,... | collective-permute-start | bytes 393224 | tf_op jit(solution)/shard_map/ppermute | solution.py:61
  59.9 5.4 %collective-permute-start.19 = (f32[8,128]{1,0:T(8,128)S(1)}, f32[8,128]{1,0:T(8,128)S(1)}, u32[]{:S(2)}, u32[]{:S(2)}) collective-permute-start(f32[8,128]{1,0:T(8,128)S(1)} %max.24), channel_id=1, source_target_pairs={{0,248},{8,0},{16,8},{24,16},{32,24},{40,32},{48,40},{56,48},{64,5... | collective-permute-start | bytes 12296 | tf_op jit(solution)/shard_map/ppermute | solution.py:61
  65.3 1.2 collective-permute-done.25
  66.6 1.9 %collective-permute-start.32 = (bf16[384,256]{1,0:T(8,128)(2,1)S(1)}, bf16[384,256]{1,0:T(8,128)(2,1)S(1)}, u32[]{:S(2)}, u32[]{:S(2)}) collective-permute-start(bf16[384,256]{1,0:T(8,128)(2,1)S(1)} %get-tuple-element.37), channel_id=1, source_target_pairs={{0,4},{1,5},{2,6},{3,7},{4,0},{5,1},{6,2},{7,3},{8,12},{9,13},{10,... | collective-permute-start | bytes 589832 | tf_op jit(solution)/shard_map/ppermute | solution.py:61
  68.5 10.0 %collective-permute-done.31 = bf16[384,256]{1,0:T(8,128)(2,1)S(1)} collective-permute-done((bf16[384,256]{1,0:T(8,128)(2,1)S(1)}, bf16[384,256]{1,0:T(8,128)(2,1)S(1)}, u32[]{:S(2)}, u32[]{:S(2)}) %collective-permute-start.31) | collective-permute-done | bytes 196640 | tf_op jit(solution)/shard_map/ppermute | solution.py:61
  78.5 5.8 %collective-permute-done.33 = bf16[384,256]{1,0:T(8,128)(2,1)S(1)} collective-permute-done((bf16[384,256]{1,0:T(8,128)(2,1)S(1)}, bf16[384,256]{1,0:T(8,128)(2,1)S(1)}, u32[]{:S(2)}, u32[]{:S(2)}) %collective-permute-start.33) | collective-permute-done | bytes 196640 | tf_op jit(solution)/shard_map/ppermute | solution.py:61
  85.2 7.1 %collective-permute-start.21 = (f32[8,128]{1,0:T(8,128)S(1)}, f32[8,128]{1,0:T(8,128)S(1)}, u32[]{:S(2)}, u32[]{:S(2)}) collective-permute-start(f32[8,128]{1,0:T(8,128)S(1)} %maximum_maximum_fusion.2), channel_id=1, source_target_pairs={{0,232},{8,240},{16,248},{24,0},{32,8},{40,16},{48,24},{56,32},{64... | collective-permute-start | bytes 12296 | tf_op jit(solution)/shard_map/ppermute | solution.py:61
  92.3 1.6 %collective-permute-done.20 = f32[8,128]{1,0:T(8,128)S(1)} collective-permute-done((f32[8,128]{1,0:T(8,128)S(1)}, f32[8,128]{1,0:T(8,128)S(1)}, u32[]{:S(2)}, u32[]{:S(2)}) %collective-permute-start.20) | collective-permute-done | bytes 4128 | tf_op jit(solution)/shard_map/ppermute | solution.py:61
  93.9 5.6 %collective-permute-start.23 = (f32[8,128]{1,0:T(8,128)S(1)}, f32[8,128]{1,0:T(8,128)S(1)}, u32[]{:S(2)}, u32[]{:S(2)}) collective-permute-start(f32[8,128]{1,0:T(8,128)S(1)} %maximum_maximum_fusion.1), channel_id=1, source_target_pairs={{0,184},{8,192},{16,200},{24,208},{32,216},{40,224},{48,232},{56,2... | collective-permute-start | bytes 12296 | tf_op jit(solution)/shard_map/ppermute | solution.py:61
  99.5 1.6 %collective-permute-done.22 = f32[8,128]{1,0:T(8,128)S(1)} collective-permute-done((f32[8,128]{1,0:T(8,128)S(1)}, f32[8,128]{1,0:T(8,128)S(1)}, u32[]{:S(2)}, u32[]{:S(2)}) %collective-permute-start.22) | collective-permute-done | bytes 4128 | tf_op jit(solution)/shard_map/ppermute | solution.py:61
  101.1 3.8 %collective-permute-start.36 = (bf16[128,512]{1,0:T(8,128)(2,1)S(1)}, bf16[128,512]{1,0:T(8,128)(2,1)S(1)}, u32[]{:S(2)}, u32[]{:S(2)}) collective-permute-start(bf16[128,512]{1,0:T(8,128)(2,1)S(1)} %get-tuple-element.33.row_here), channel_id=1, source_target_pairs={{0,248},{8,0},{16,8},{24,16},{32,24},{40,32},{48,40},{56,48},{64,5... | collective-permute-start | bytes 393224 | tf_op jit(solution)/shard_map/ppermute | solution.py:61
  104.9 7.5 %collective-permute-done.24 = f32[8,128]{1,0:T(8,128)S(1)} collective-permute-done((f32[8,128]{1,0:T(8,128)S(1)}, f32[8,128]{1,0:T(8,128)S(1)}, u32[]{:S(2)}, u32[]{:S(2)}) %collective-permute-start.24) | collective-permute-done | bytes 4128 | tf_op jit(solution)/shard_map/ppermute | solution.py:61
  112.4 10.1 %shard_map.78 = (bf16[128,512]{1,0:T(8,128)(2,1)S(1)}, f32[128,512]{1,0:T(8,128)S(1)}, bf16[128,512]{1,0:T(8,128)(2,1)S(1)}) custom-call(s32[1,3,2,2]{3,2,1,0:T(2,128)S(1)} %copy.9.pair, f32[8,128]{1,0:T(8,128)S(1)} %max.31.peak, bf16[1024,256]{1,0:T(8,128)(2,1)S(1)} %constant_dynamic-update-slice_fusion.own_mine, ...), custom_call_target="tpu_custom_call" | custom-call | flops 5637144576 | bytes 3543088 | tf_op jit(solution)/shard_map/pallas_call | solution.py:44
  122.7 5.3 %collective-permute-start.38 = (bf16[128,512]{1,0:T(8,128)(2,1)S(1)}, bf16[128,512]{1,0:T(8,128)(2,1)S(1)}, u32[]{:S(2)}, u32[]{:S(2)}) collective-permute-start(bf16[128,512]{1,0:T(8,128)(2,1)S(1)} %get-tuple-element.36), channel_id=1, source_target_pairs={{0,248},{8,0},{16,8},{24,16},{32,24},{40,32},{48,40},{56,48},{64,5... | collective-permute-start | bytes 393224 | tf_op jit(solution)/shard_map/ppermute | solution.py:61
  128.0 2.9 %collective-permute-done.37.before = bf16[128,512]{1,0:T(8,128)(2,1)S(1)} collective-permute-done((bf16[128,512]{1,0:T(8,128)(2,1)S(1)}, bf16[128,512]{1,0:T(8,128)(2,1)S(1)}, u32[]{:S(2)}, u32[]{:S(2)}) %collective-permute-start.37) | collective-permute-done | bytes 131104 | tf_op jit(solution)/shard_map/ppermute | solution.py:61
  (83 shorter events, 12.8 us)
Async XLA Ops:
  2.2 9.3 %collective-permute-start.1 = (bf16[128,512]{1,0:T(8,128)(2,1)S(1)}, bf16[128,512]{1,0:T(8,128)(2,1)S(1)}, u32[]{:S(2)}, u32[]{:S(2)}) collective-permute-start(bf16[128,512]{1,0:T(8,128)(2,1)S(1)} %shard_map.74.t0), channel_id=1, source_target_pairs={{0,6},{1,7},{2,0},{3,1},{4,2},{5,3},{6,4},{7,5},{8,14},{9,15},{10,... | collective-permute-start | bytes 393224 | tf_op jit(solution)/shard_map/ppermute | solution.py:61
  3.0 8.5 %collective-permute-start.2 = (bf16[128,512]{1,0:T(8,128)(2,1)S(1)}, bf16[128,512]{1,0:T(8,128)(2,1)S(1)}, u32[]{:S(2)}, u32[]{:S(2)}) collective-permute-start(bf16[128,512]{1,0:T(8,128)(2,1)S(1)} %shard_map.74.t0), channel_id=1, source_target_pairs={{0,4},{1,5},{2,6},{3,7},{4,0},{5,1},{6,2},{7,3},{8,12},{9,13},{10,... | collective-permute-start | bytes 393224 | tf_op jit(solution)/shard_map/ppermute | solution.py:61
  12.5 22.2 %collective-permute-start.13 = (bf16[128,2048]{1,0:T(8,128)(2,1)S(1)}, bf16[128,2048]{1,0:T(8,128)(2,1)S(1)}, u32[]{:S(2)}, u32[]{:S(2)}) collective-permute-start(bf16[128,2048]{1,0:T(8,128)(2,1)S(1)} %get-tuple-element.25.m_own), channel_id=1, source_target_pairs={{0,1},{1,0},{2,3},{3,2},{4,5},{5,4},{6,7},{7,6},{8,9},{9,8},{10,11... | collective-permute-start | bytes 1572872 | tf_op jit(solution)/shard_map/ppermute | solution.py:66
  14.1 11.9 %collective-permute-start.8 = (bf16[256,256]{1,0:T(8,128)(2,1)S(1)}, bf16[256,256]{1,0:T(8,128)(2,1)S(1)}, u32[]{:S(2)}, u32[]{:S(2)}) collective-permute-start(bf16[256,256]{1,0:T(8,128)(2,1)S(1)} %add_convert_fusion.p0), channel_id=1, source_target_pairs={{0,8},{8,16},{16,24},{24,32},{32,40},{40,48},{48,56},{56,64},{64,7... | collective-permute-start | bytes 393224 | tf_op jit(solution)/shard_map/ppermute | solution.py:61
  16.1 12.6 %collective-permute-start.12 = (bf16[256,256]{1,0:T(8,128)(2,1)S(1)}, bf16[256,256]{1,0:T(8,128)(2,1)S(1)}, u32[]{:S(2)}, u32[]{:S(2)}) collective-permute-start(bf16[256,256]{1,0:T(8,128)(2,1)S(1)} %add_convert_fusion.p0), channel_id=1, source_target_pairs={{0,1},{1,0},{2,3},{3,2},{4,5},{5,4},{6,7},{7,6},{8,9},{9,8},{10,11... | collective-permute-start | bytes 393224 | tf_op jit(solution)/shard_map/ppermute | solution.py:66
  16.1 12.6 %collective-permute-start.5 = (bf16[256,256]{1,0:T(8,128)(2,1)S(1)}, bf16[256,256]{1,0:T(8,128)(2,1)S(1)}, u32[]{:S(2)}, u32[]{:S(2)}) collective-permute-start(bf16[256,256]{1,0:T(8,128)(2,1)S(1)} %add_convert_fusion.p0), channel_id=1, source_target_pairs={{0,6},{1,7},{2,0},{3,1},{4,2},{5,3},{6,4},{7,5},{8,14},{9,15},{10,... | collective-permute-start | bytes 393224 | tf_op jit(solution)/shard_map/ppermute | solution.py:61
  16.7 14.0 %collective-permute-start.6 = (bf16[256,256]{1,0:T(8,128)(2,1)S(1)}, bf16[256,256]{1,0:T(8,128)(2,1)S(1)}, u32[]{:S(2)}, u32[]{:S(2)}) collective-permute-start(bf16[256,256]{1,0:T(8,128)(2,1)S(1)} %add_convert_fusion.p0), channel_id=1, source_target_pairs={{0,4},{1,5},{2,6},{3,7},{4,0},{5,1},{6,2},{7,3},{8,12},{9,13},{10,... | collective-permute-start | bytes 393224 | tf_op jit(solution)/shard_map/ppermute | solution.py:61
  26.0 8.7 %collective-permute-start.7 = (bf16[256,256]{1,0:T(8,128)(2,1)S(1)}, bf16[256,256]{1,0:T(8,128)(2,1)S(1)}, u32[]{:S(2)}, u32[]{:S(2)}) collective-permute-start(bf16[256,256]{1,0:T(8,128)(2,1)S(1)} %add_convert_fusion.p0), channel_id=1, source_target_pairs={{0,2},{1,3},{2,4},{3,5},{4,6},{5,7},{6,0},{7,1},{8,10},{9,11},{10,... | collective-permute-start | bytes 393224 | tf_op jit(solution)/shard_map/ppermute | solution.py:61
  28.7 7.7 %collective-permute-start.10 = (bf16[256,256]{1,0:T(8,128)(2,1)S(1)}, bf16[256,256]{1,0:T(8,128)(2,1)S(1)}, u32[]{:S(2)}, u32[]{:S(2)}) collective-permute-start(bf16[256,256]{1,0:T(8,128)(2,1)S(1)} %collective-permute-done.8.q0), channel_id=1, source_target_pairs={{0,4},{1,5},{2,6},{3,7},{4,0},{5,1},{6,2},{7,3},{8,12},{9,13},{10,... | collective-permute-start | bytes 393224 | tf_op jit(solution)/shard_map/ppermute | solution.py:61
  28.7 8.1 %collective-permute-start.11 = (bf16[256,256]{1,0:T(8,128)(2,1)S(1)}, bf16[256,256]{1,0:T(8,128)(2,1)S(1)}, u32[]{:S(2)}, u32[]{:S(2)}) collective-permute-start(bf16[256,256]{1,0:T(8,128)(2,1)S(1)} %collective-permute-done.8.q0), channel_id=1, source_target_pairs={{0,2},{1,3},{2,4},{3,5},{4,6},{5,7},{6,0},{7,1},{8,10},{9,11},{10,... | collective-permute-start | bytes 393224 | tf_op jit(solution)/shard_map/ppermute | solution.py:61
  39.2 8.2 %collective-permute-start.14 = (bf16[272,256]{1,0:T(8,128)(2,1)S(1)}, bf16[272,256]{1,0:T(8,128)(2,1)S(1)}, u32[]{:S(2)}, u32[]{:S(2)}) collective-permute-start(bf16[272,256]{1,0:T(8,128)(2,1)S(1)} %get-tuple-element.27), channel_id=1, source_target_pairs={{0,2},{1,3},{2,4},{3,5},{4,6},{5,7},{6,0},{7,1},{8,10},{9,11},{10,... | collective-permute-start | bytes 417800 | tf_op jit(solution)/shard_map/ppermute | solution.py:61
  42.1 7.6 %collective-permute-start.15 = (bf16[272,256]{1,0:T(8,128)(2,1)S(1)}, bf16[272,256]{1,0:T(8,128)(2,1)S(1)}, u32[]{:S(2)}, u32[]{:S(2)}) collective-permute-start(bf16[272,256]{1,0:T(8,128)(2,1)S(1)} %get-tuple-element.28), channel_id=1, source_target_pairs={{0,4},{1,5},{2,6},{3,7},{4,0},{5,1},{6,2},{7,3},{8,12},{9,13},{10,... | collective-permute-start | bytes 417800 | tf_op jit(solution)/shard_map/ppermute | solution.py:61
  42.1 8.7 %collective-permute-start.16 = (bf16[272,256]{1,0:T(8,128)(2,1)S(1)}, bf16[272,256]{1,0:T(8,128)(2,1)S(1)}, u32[]{:S(2)}, u32[]{:S(2)}) collective-permute-start(bf16[272,256]{1,0:T(8,128)(2,1)S(1)} %get-tuple-element.29), channel_id=1, source_target_pairs={{0,6},{1,7},{2,0},{3,1},{4,2},{5,3},{6,4},{7,5},{8,14},{9,15},{10,... | collective-permute-start | bytes 417800 | tf_op jit(solution)/shard_map/ppermute | solution.py:61
  51.1 8.8 %collective-permute-start.29 = (bf16[128,256]{1,0:T(8,128)(2,1)S(1)}, bf16[128,256]{1,0:T(8,128)(2,1)S(1)}, u32[]{:S(2)}, u32[]{:S(2)}) collective-permute-start(bf16[128,256]{1,0:T(8,128)(2,1)S(1)} %get-tuple-element.32), channel_id=1, source_target_pairs={{0,8},{8,16},{16,24},{24,32},{32,40},{40,48},{48,56},{56,64},{64,7... | collective-permute-start | bytes 196616 | tf_op jit(solution)/shard_map/ppermute | solution.py:61
  51.2 8.7 %collective-permute-start.30 = (bf16[256,256]{1,0:T(8,128)(2,1)S(1)}, bf16[256,256]{1,0:T(8,128)(2,1)S(1)}, u32[]{:S(2)}, u32[]{:S(2)}) collective-permute-start(bf16[256,256]{1,0:T(8,128)(2,1)S(1)} %get-tuple-element.31), channel_id=1, source_target_pairs={{0,248},{8,0},{16,8},{24,16},{32,24},{40,32},{48,40},{56,48},{64,5... | collective-permute-start | bytes 393224 | tf_op jit(solution)/shard_map/ppermute | solution.py:61
  56.5 10.0 %collective-permute-start.25 = (bf16[256,256]{1,0:T(8,128)(2,1)S(1)}, bf16[256,256]{1,0:T(8,128)(2,1)S(1)}, u32[]{:S(2)}, u32[]{:S(2)}) collective-permute-start(bf16[256,256]{1,0:T(8,128)(2,1)S(1)} %get-tuple-element.31), channel_id=1, source_target_pairs={{0,6},{1,7},{2,0},{3,1},{4,2},{5,3},{6,4},{7,5},{8,14},{9,15},{10,... | collective-permute-start | bytes 393224 | tf_op jit(solution)/shard_map/ppermute | solution.py:61
  56.6 10.0 %collective-permute-start.26 = (bf16[256,256]{1,0:T(8,128)(2,1)S(1)}, bf16[256,256]{1,0:T(8,128)(2,1)S(1)}, u32[]{:S(2)}, u32[]{:S(2)}) collective-permute-start(bf16[256,256]{1,0:T(8,128)(2,1)S(1)} %get-tuple-element.31), channel_id=1, source_target_pairs={{0,4},{1,5},{2,6},{3,7},{4,0},{5,1},{6,2},{7,3},{8,12},{9,13},{10,... | collective-permute-start | bytes 393224 | tf_op jit(solution)/shard_map/ppermute | solution.py:61
  59.0 25.5 %collective-permute-start.27 = (bf16[256,256]{1,0:T(8,128)(2,1)S(1)}, bf16[256,256]{1,0:T(8,128)(2,1)S(1)}, u32[]{:S(2)}, u32[]{:S(2)}) collective-permute-start(bf16[256,256]{1,0:T(8,128)(2,1)S(1)} %get-tuple-element.31), channel_id=1, source_target_pairs={{0,2},{1,3},{2,4},{3,5},{4,6},{5,7},{6,0},{7,1},{8,10},{9,11},{10,... | collective-permute-start | bytes 393224 | tf_op jit(solution)/shard_map/ppermute | solution.py:61
  59.8 25.2 %collective-permute-start.18 = (f32[8,128]{1,0:T(8,128)S(1)}, f32[8,128]{1,0:T(8,128)S(1)}, u32[]{:S(2)}, u32[]{:S(2)}) collective-permute-start(f32[8,128]{1,0:T(8,128)S(1)} %max.24), channel_id=1, source_target_pairs={{0,8},{8,16},{16,24},{24,32},{32,40},{40,48},{48,56},{56,64},{64,7... | collective-permute-start | bytes 12296 | tf_op jit(solution)/shard_map/ppermute | solution.py:61
  59.9 25.2 %collective-permute-start.19 = (f32[8,128]{1,0:T(8,128)S(1)}, f32[8,128]{1,0:T(8,128)S(1)}, u32[]{:S(2)}, u32[]{:S(2)}) collective-permute-start(f32[8,128]{1,0:T(8,128)S(1)} %max.24), channel_id=1, source_target_pairs={{0,248},{8,0},{16,8},{24,16},{32,24},{40,32},{48,40},{56,48},{64,5... | collective-permute-start | bytes 12296 | tf_op jit(solution)/shard_map/ppermute | solution.py:61
  66.5 12.0 %collective-permute-start.31 = (bf16[384,256]{1,0:T(8,128)(2,1)S(1)}, bf16[384,256]{1,0:T(8,128)(2,1)S(1)}, u32[]{:S(2)}, u32[]{:S(2)}) collective-permute-start(bf16[384,256]{1,0:T(8,128)(2,1)S(1)} %get-tuple-element.37), channel_id=1, source_target_pairs={{0,6},{1,7},{2,0},{3,1},{4,2},{5,3},{6,4},{7,5},{8,14},{9,15},{10,... | collective-permute-start | bytes 589832 | tf_op jit(solution)/shard_map/ppermute | solution.py:61
  66.6 11.9 %collective-permute-start.32 = (bf16[384,256]{1,0:T(8,128)(2,1)S(1)}, bf16[384,256]{1,0:T(8,128)(2,1)S(1)}, u32[]{:S(2)}, u32[]{:S(2)}) collective-permute-start(bf16[384,256]{1,0:T(8,128)(2,1)S(1)} %get-tuple-element.37), channel_id=1, source_target_pairs={{0,4},{1,5},{2,6},{3,7},{4,0},{5,1},{6,2},{7,3},{8,12},{9,13},{10,... | collective-permute-start | bytes 589832 | tf_op jit(solution)/shard_map/ppermute | solution.py:61
  84.4 28.1 %collective-permute-start.34 = (bf16[1536,256]{1,0:T(8,128)(2,1)S(1)}, bf16[1536,256]{1,0:T(8,128)(2,1)S(1)}, u32[]{:S(2)}, u32[]{:S(2)}) collective-permute-start(bf16[1536,256]{1,0:T(8,128)(2,1)S(1)} %constant_dynamic-update-slice_fusion.6.near_mine), channel_id=1, source_target_pairs={{0,1},{1,0},{2,3},{3,2},{4,5},{5,4},{6,7},{7,6},{8,9},{9,8},{10,11... | collective-permute-start | bytes 2359304 | tf_op jit(solution)/shard_map/ppermute | solution.py:66
  84.5 27.9 %collective-permute-start.28 = (bf16[1024,256]{1,0:T(8,128)(2,1)S(1)}, bf16[1024,256]{1,0:T(8,128)(2,1)S(1)}, u32[]{:S(2)}, u32[]{:S(2)}) collective-permute-start(bf16[1024,256]{1,0:T(8,128)(2,1)S(1)} %constant_dynamic-update-slice_fusion.own_mine), channel_id=1, source_target_pairs={{0,1},{1,0},{2,3},{3,2},{4,5},{5,4},{6,7},{7,6},{8,9},{9,8},{10,11... | collective-permute-start | bytes 1572872 | tf_op jit(solution)/shard_map/ppermute | solution.py:66
  85.1 8.8 %collective-permute-start.20 = (f32[8,128]{1,0:T(8,128)S(1)}, f32[8,128]{1,0:T(8,128)S(1)}, u32[]{:S(2)}, u32[]{:S(2)}) collective-permute-start(f32[8,128]{1,0:T(8,128)S(1)} %maximum_maximum_fusion.2), channel_id=1, source_target_pairs={{0,24},{8,32},{16,40},{24,48},{32,56},{40,64},{48,72},{56,80},{64,... | collective-permute-start | bytes 12296 | tf_op jit(solution)/shard_map/ppermute | solution.py:61
  85.2 8.7 %collective-permute-start.21 = (f32[8,128]{1,0:T(8,128)S(1)}, f32[8,128]{1,0:T(8,128)S(1)}, u32[]{:S(2)}, u32[]{:S(2)}) collective-permute-start(f32[8,128]{1,0:T(8,128)S(1)} %maximum_maximum_fusion.2), channel_id=1, source_target_pairs={{0,232},{8,240},{16,248},{24,0},{32,8},{40,16},{48,24},{56,32},{64... | collective-permute-start | bytes 12296 | tf_op jit(solution)/shard_map/ppermute | solution.py:61
  93.9 11.0 %collective-permute-start.23 = (f32[8,128]{1,0:T(8,128)S(1)}, f32[8,128]{1,0:T(8,128)S(1)}, u32[]{:S(2)}, u32[]{:S(2)}) collective-permute-start(f32[8,128]{1,0:T(8,128)S(1)} %maximum_maximum_fusion.1), channel_id=1, source_target_pairs={{0,184},{8,192},{16,200},{24,208},{32,216},{40,224},{48,232},{56,2... | collective-permute-start | bytes 12296 | tf_op jit(solution)/shard_map/ppermute | solution.py:61
  99.5 12.9 %collective-permute-start.35 = (bf16[128,512]{1,0:T(8,128)(2,1)S(1)}, bf16[128,512]{1,0:T(8,128)(2,1)S(1)}, u32[]{:S(2)}, u32[]{:S(2)}) collective-permute-start(bf16[128,512]{1,0:T(8,128)(2,1)S(1)} %get-tuple-element.33.row_here), channel_id=1, source_target_pairs={{0,8},{8,16},{16,24},{24,32},{32,40},{40,48},{48,56},{56,64},{64,7... | collective-permute-start | bytes 393224 | tf_op jit(solution)/shard_map/ppermute | solution.py:61
  101.1 11.3 %collective-permute-start.36 = (bf16[128,512]{1,0:T(8,128)(2,1)S(1)}, bf16[128,512]{1,0:T(8,128)(2,1)S(1)}, u32[]{:S(2)}, u32[]{:S(2)}) collective-permute-start(bf16[128,512]{1,0:T(8,128)(2,1)S(1)} %get-tuple-element.33.row_here), channel_id=1, source_target_pairs={{0,248},{8,0},{16,8},{24,16},{32,24},{40,32},{48,40},{56,48},{64,5... | collective-permute-start | bytes 393224 | tf_op jit(solution)/shard_map/ppermute | solution.py:61
  104.9 7.5 %collective-permute-start.24 = (f32[8,128]{1,0:T(8,128)S(1)}, f32[8,128]{1,0:T(8,128)S(1)}, u32[]{:S(2)}, u32[]{:S(2)}) collective-permute-start(f32[8,128]{1,0:T(8,128)S(1)} %maximum_maximum_fusion), channel_id=1, source_target_pairs={{0,40},{8,48},{16,56},{24,64},{32,72},{40,80},{48,88},{56,96},{64,... | collective-permute-start | bytes 12296 | tf_op jit(solution)/shard_map/ppermute | solution.py:61
  122.6 8.4 %collective-permute-start.37 = (bf16[128,512]{1,0:T(8,128)(2,1)S(1)}, bf16[128,512]{1,0:T(8,128)(2,1)S(1)}, u32[]{:S(2)}, u32[]{:S(2)}) collective-permute-start(bf16[128,512]{1,0:T(8,128)(2,1)S(1)} %get-tuple-element.34), channel_id=1, source_target_pairs={{0,8},{8,16},{16,24},{24,32},{32,40},{40,48},{48,56},{56,64},{64,7... | collective-permute-start | bytes 393224 | tf_op jit(solution)/shard_map/ppermute | solution.py:61
  122.7 8.3 %collective-permute-start.38 = (bf16[128,512]{1,0:T(8,128)(2,1)S(1)}, bf16[128,512]{1,0:T(8,128)(2,1)S(1)}, u32[]{:S(2)}, u32[]{:S(2)}) collective-permute-start(bf16[128,512]{1,0:T(8,128)(2,1)S(1)} %get-tuple-element.36), channel_id=1, source_target_pairs={{0,248},{8,0},{16,8},{24,16},{32,24},{40,32},{48,40},{56,48},{64,5... | collective-permute-start | bytes 393224 | tf_op jit(solution)/shard_map/ppermute | solution.py:61
  (14 other events, 64.8 us)
